TPU v7x, 32 devices: a whole 2x2x4 slice. The times are simulated.
32 devices in a mesh: grp: 2 (over y), par: 8 (over z, x), smp: 2 (over core).
Axes of the slice: x: 2, y: 2, z: 4, core: 2. Of those that a mesh axis runs over, the one named last changes fastest.
Arguments:
- log_derivs: bfloat16 [2048, 524288], P(('grp', 'smp'), 'par'), parts along dimension 0, may hold values from -2000 to 2000, as said below
- spin_states: int32 [2048, 100], P(('grp', 'smp')), parts along dimension 0, may hold values from 0 to 1
- offdiag_energy: float32 [2048], P(('grp', 'smp')), parts along dimension 0, may hold values from -24 to 24
Outputs:
- param_update: float32 [1048576], P(('grp', 'par', 'smp')), parts along dimension 0
- coefficients: float32 [2048], P('grp'), parts along dimension 0
There are 2 independent parts, one for each index of `grp`. A program takes and returns all parts, laid end to end along the dimension named above; each array names one. Nothing has to cross between parts.
Inputs may be any that keep to these rules, and one draw needn't show every extreme that they name: `log_derivs`: real values.
All inputs are finite; a program needn't handle non-finite values.
Results may differ from a plain program's by a relative error of at most 0.0031.
Values may be sent and summed in bfloat16 or wider, within the bound.
A program may use at most 512 MiB of HBM per device.

v0:
```python
import math

import jax
import jax.numpy as jnp
from jax import lax
from jax.sharding import PartitionSpec as P

NP = 524288
SIDE = 10


near_coupling = 1.0
diagonal_coupling = 0.5
damp_ratio = 0.05


def lattice_energy(spin_states):
    signs = (2 * spin_states - 1).astype(jnp.float32).reshape(spin_states.shape[0], SIDE, SIDE)
    nearest = signs * jnp.roll(signs, -1, 1) + signs * jnp.roll(signs, -1, 2)
    shifted = jnp.roll(signs, -1, 1)
    diagonal_pairs = signs * jnp.roll(shifted, -1, 2) + signs * jnp.roll(shifted, 1, 2)
    return near_coupling * jnp.sum(nearest, axis=(1, 2)) + diagonal_coupling * jnp.sum(
        diagonal_pairs, axis=(1, 2)
    )


def row_products(left, right):
    return lax.dot_general(
        left, right, (((1,), (1,)), ((), ())), preferred_element_type=jnp.float32
    )


def solve_system(gram_matrix, energies):
    matrix_order = gram_matrix.shape[0]
    centred_energy = energies - jnp.sum(energies) / matrix_order
    damping = damp_ratio * jnp.trace(gram_matrix) / matrix_order
    system = gram_matrix + damping * jnp.eye(matrix_order, dtype=jnp.float32)
    factor = jnp.linalg.cholesky(system)
    return jax.scipy.linalg.cho_solve((factor, True), centred_energy)


def back_project(weights, centred, total_rows):
    return -jnp.dot(
        weights,
        centred.astype(jnp.float32),
        precision=lax.Precision.HIGHEST,
        preferred_element_type=jnp.float32,
    ) / math.sqrt(total_rows)


def local(log_derivs, spin_states, offdiag_energy):
    row_count = log_derivs.shape[0]
    total_rows = row_count * lax.axis_size("smp")
    local_energy = lattice_energy(spin_states) + offdiag_energy
    col_sums = lax.psum(jnp.sum(log_derivs.astype(jnp.float32), axis=0), "smp")
    centred = (log_derivs.astype(jnp.float32) - (col_sums / total_rows)[None, :]).astype(
        jnp.bfloat16
    )
    partial_rows = row_products(centred, lax.all_gather(centred, "smp", axis=0, tiled=True))
    gram_block = lax.psum(partial_rows, "par") / NP
    gram_matrix, energies = (
        lax.all_gather(gram_block, "smp", axis=0, tiled=True),
        lax.all_gather(local_energy, "smp", axis=0, tiled=True),
    )
    coefficients = solve_system(gram_matrix, energies)
    first_row = lax.axis_index("smp") * row_count
    own_coeffs = lax.dynamic_slice_in_dim(coefficients, first_row, row_count, 0)
    partial_update = back_project(own_coeffs, centred, total_rows)
    param_update = lax.psum_scatter(partial_update, "smp", scatter_dimension=0, tiled=True)
    return (param_update, coefficients)


def solution(mesh):
    placed = (P(("grp", "smp"), "par"), P(("grp", "smp"), None), P(("grp", "smp")))
    return jax.shard_map(
        local,
        mesh=mesh,
        in_specs=placed,
        out_specs=(P(("grp", "par", "smp")), P("grp")),
        check_vma=False,
    )
```

profile of v0, /device:TPU:0, one launch (start us, length us, event | category | flops | bytes accessed | tf_op | source)
XLA Modules:
  0.0 898.6 jit_solution(9401822934235452654)
XLA Ops:
  7.2 21.6 %convert_reduce_fusion = f32[65536]{0:T(1024)} fusion(bf16[512,65536]{1,0:T(8,128)(2,1)} %param.3), kind=kLoop, calls=%fused_computation.3 | loop fusion | flops 67043328 | bytes 67371008 | tf_op jit(solution)/shard_map/reduce_sum | solution.py:55
  28.8 21.1 %all-reduce.6.cloned.1.call-done = f32[65536]{0:T(1024)} async-done(((f32[65536]{0:T(1024)}), f32[65536]{0:T(1024)}) %all-reduce.6.cloned.1.call-update) | async-done | bytes 262160 | tf_op jit(solution)/shard_map/psum | solution.py:55
  50.9 44.8 %fusion = bf16[512,65536]{1,0:T(8,128)(2,1)} fusion(bf16[512,65536]{1,0:T(8,128)(2,1)} %param.3, f32[65536]{0:T(1024)S(1)} %broadcast_multiply_fusion.1), kind=kLoop, calls=%fused_computation.4 | loop fusion | flops 100663296 | bytes 134479872 | tf_op jit(solution)/shard_map/convert_element_type | solution.py:56
  95.8 184.1 %all-gather.4.cloned.1.call-done = bf16[1024,65536]{1,0:T(8,128)(2,1)} async-done(((bf16[512,65536]{1,0:T(8,128)(2,1)}), bf16[1024,65536]{1,0:T(8,128)(2,1)}) %all-gather.4.cloned.1.call-update) | async-done | bytes 134217744 | tf_op jit(solution)/shard_map/all_gather | solution.py:59
  279.9 81.2 %fusion.127 = f32[512,1024]{0,1:T(8,128)} fusion(bf16[512,65536]{1,0:T(8,128)(2,1)} %fusion, bf16[1024,65536]{1,0:T(8,128)(2,1)} %all-gather.4.cloned.1.call-done), kind=kOutput, calls=%fused_computation.274 | convolution fusion | flops 68719476736 | bytes 203423744 | tf_op jit(solution)/shard_map/dot_general | solution.py:28
  361.2 103.1 %all-reduce.8.cloned.1.call-done = f32[512,1024]{0,1:T(8,128)} async-done(((f32[512,1024]{0,1:T(8,128)}), f32[512,1024]{0,1:T(8,128)}) %all-reduce.8.cloned.1.call-update) | async-done | bytes 2097168 | tf_op jit(solution)/shard_map/psum | solution.py:60
  464.3 3.2 broadcast_multiply_fusion
  468.2 1.8 all-gather
  471.3 9.8 %all-gather.6.cloned.1.call-done = f32[1024,1024]{0,1:T(8,128)} async-done(((f32[512,1024]{0,1:T(8,128)}), f32[1024,1024]{0,1:T(8,128)}) %all-gather.6.cloned.1.call-update) | async-done | bytes 4194320 | tf_op jit(solution)/shard_map/all_gather | solution.py:62
  481.0 2.9 select_reduce_fusion
  484.6 4.8 select_add_fusion
  489.5 5.5 copy.24
  495.0 4.5 fusion.1
  499.4 1.9 copy-done
  501.4 11.7 %cholesky.222 = f32[128,128]{1,0:T(8,128)S(1)} custom-call(f32[128,128]{1,0:T(8,128)S(1)} %cholesky.577), custom_call_target="Cholesky" | custom-call | tf_op jit(solution)/shard_map/jit(cholesky)/cholesky | solution.py:38
  513.1 9.8 %custom-call.66 = f32[1,128,128]{1,2,0:T(8,128)S(1)} custom-call(f32[1,128,128]{2,1,0:T(8,128)S(1)} %get-tuple-element.47), custom_call_target="InvertDiagBlocksLowerTriangular" | custom-call | tf_op jit(solution)/shard_map/jit(cholesky)/cholesky | solution.py:38
  522.9 1.5 fusion.39
  524.5 1.6 convolution_subtract_fusion
  526.0 11.7 %cholesky.243 = f32[128,128]{1,0:T(8,128)S(1)} custom-call(f32[128,128]{1,0:T(8,128)S(1)} %cholesky.581), custom_call_target="Cholesky" | custom-call | tf_op jit(solution)/shard_map/jit(cholesky)/cholesky | solution.py:38
  538.4 2.5 cholesky.254
  540.9 9.8 %custom-call.67 = f32[1,128,128]{1,2,0:T(8,128)S(1)} custom-call(f32[1,128,128]{2,1,0:T(8,128)S(1)} %get-tuple-element.45), custom_call_target="InvertDiagBlocksLowerTriangular" | custom-call | tf_op jit(solution)/shard_map/jit(cholesky)/cholesky | solution.py:38
  552.2 1.3 convolution_dynamic-update-slice_fusion
  553.5 2.7 convolution_subtract_fusion.1
  556.2 11.7 %cholesky.466 = f32[128,128]{1,0:T(8,128)S(1)} custom-call(f32[128,128]{1,0:T(8,128)S(1)} %cholesky.586), custom_call_target="Cholesky" | custom-call | tf_op jit(solution)/shard_map/jit(cholesky)/cholesky | solution.py:38
  568.7 9.8 %custom-call.68 = f32[1,128,128]{1,2,0:T(8,128)S(1)} custom-call(f32[1,128,128]{2,1,0:T(8,128)S(1)} %get-tuple-element.43), custom_call_target="InvertDiagBlocksLowerTriangular" | custom-call | tf_op jit(solution)/shard_map/jit(cholesky)/cholesky | solution.py:38
  578.5 1.3 convolution_dynamic-update-slice_fusion.1
  579.7 3.5 convolution_subtract_fusion.2
  583.3 11.7 %cholesky.485 = f32[128,128]{1,0:T(8,128)S(1)} custom-call(f32[128,128]{1,0:T(8,128)S(1)} %cholesky.591), custom_call_target="Cholesky" | custom-call | tf_op jit(solution)/shard_map/jit(cholesky)/cholesky | solution.py:38
  595.8 9.8 %custom-call.69 = f32[1,128,128]{1,2,0:T(8,128)S(1)} custom-call(f32[1,128,128]{2,1,0:T(8,128)S(1)} %get-tuple-element.41), custom_call_target="InvertDiagBlocksLowerTriangular" | custom-call | tf_op jit(solution)/shard_map/jit(cholesky)/cholesky | solution.py:38
  606.7 3.1 convolution_subtract_fusion.3
  609.9 11.8 %cholesky.504 = f32[128,128]{1,0:T(8,128)S(1)} custom-call(f32[128,128]{1,0:T(8,128)S(1)} %cholesky.596), custom_call_target="Cholesky" | custom-call | tf_op jit(solution)/shard_map/jit(cholesky)/cholesky | solution.py:38
  622.5 9.8 %custom-call.70 = f32[1,128,128]{1,2,0:T(8,128)S(1)} custom-call(f32[1,128,128]{2,1,0:T(8,128)S(1)} %get-tuple-element.39), custom_call_target="InvertDiagBlocksLowerTriangular" | custom-call | tf_op jit(solution)/shard_map/jit(cholesky)/cholesky | solution.py:38
  633.5 3.1 convolution_subtract_fusion.4
  636.5 11.7 %cholesky.524 = f32[128,128]{1,0:T(8,128)S(1)} custom-call(f32[128,128]{1,0:T(8,128)S(1)} %cholesky.601), custom_call_target="Cholesky" | custom-call | tf_op jit(solution)/shard_map/jit(cholesky)/cholesky | solution.py:38
  649.0 9.8 %custom-call.71 = f32[1,128,128]{1,2,0:T(8,128)S(1)} custom-call(f32[1,128,128]{2,1,0:T(8,128)S(1)} %get-tuple-element.37), custom_call_target="InvertDiagBlocksLowerTriangular" | custom-call | tf_op jit(solution)/shard_map/jit(cholesky)/cholesky | solution.py:38
  659.8 2.9 convolution_subtract_fusion.5
  662.7 11.7 %cholesky.544 = f32[128,128]{1,0:T(8,128)S(1)} custom-call(f32[128,128]{1,0:T(8,128)S(1)} %cholesky.606), custom_call_target="Cholesky" | custom-call | tf_op jit(solution)/shard_map/jit(cholesky)/cholesky | solution.py:38
  675.2 9.8 %custom-call.72 = f32[1,128,128]{1,2,0:T(8,128)S(1)} custom-call(f32[1,128,128]{2,1,0:T(8,128)S(1)} %get-tuple-element.35), custom_call_target="InvertDiagBlocksLowerTriangular" | custom-call | tf_op jit(solution)/shard_map/jit(cholesky)/cholesky | solution.py:38
  686.0 2.1 convolution_subtract_fusion.6
  688.0 11.7 %cholesky.562 = f32[128,128]{1,0:T(8,128)S(1)} custom-call(f32[128,128]{1,0:T(8,128)S(1)} %convolution_subtract_fusion.6), custom_call_target="Cholesky" | custom-call | tf_op jit(solution)/shard_map/jit(cholesky)/cholesky | solution.py:38
  710.1 4.8 select_select_fusion
  714.9 23.9 %while.1 = (s32[]{:T(128)}, f32[1024,1024]{0,1:T(8,128)}, s32[8,2]{0,1:T(2,128)S(1)}, f32[8,128,128]{2,1,0:T(8,128)S(1)}, s32[]{:T(128)}) while((s32[]{:T(128)}, f32[1024,1024]{0,1:T(8,128)}, s32[8,2]{0,1:T(2,128)S(1)}, f32[8,128,128]{2,1,0:T(8,128)S(1)}, s32[]{:T(128)}) %tuple.57), condition=%wide.while_cond, body=%wide.while_body.sunk | while | flops 2 | bytes 393321 | solution.py:39
  715.5 2.3 dynamic-slice.10
  718.5 2.3 dynamic-slice.10
  721.5 2.3 dynamic-slice.10
  724.5 2.3 dynamic-slice.10
  727.5 2.3 dynamic-slice.10
  730.5 2.3 dynamic-slice.10
  733.5 2.3 dynamic-slice.10
  736.5 2.2 dynamic-slice.10
  738.8 78.8 %custom-call.73 = f32[8,128,128]{1,2,0:T(8,128)S(1)} custom-call(f32[8,128,128]{2,1,0:T(8,128)S(1)} %get-tuple-element.9), custom_call_target="InvertDiagBlocksLowerTriangular" | custom-call | tf_op jit(solution)/shard_map/jit(_cho_solve)/triangular_solve | solution.py:39
  820.3 1.2 fusion.30
  821.7 1.2 fusion.16
  823.1 1.3 fusion.28
  824.5 1.3 fusion.18
  826.0 1.4 fusion.12
  830.4 1.2 fusion.26
  831.9 1.3 fusion.20
  833.5 1.4 fusion.24
  835.1 1.4 fusion.22
  836.8 1.5 fusion.14
  838.7 31.0 %fusion.98 = f32[1,65536]{1,0:T(1,128)S(1)} fusion(bf16[512,65536]{1,0:T(8,128)(2,1)} %fusion, f32[1024,1]{0,1:T(1,128)S(1)} %constant_dynamic-update-slice_fusion.36, s32[]{:T(128)S(6)} %select_n.14), kind=kOutput, calls=%fused_computation.227 | convolution fusion | flops 402653184 | bytes 67373056 | tf_op jit(solution)/shard_map/dot_general | solution.py:43
  871.7 18.3 %all-reduce.10.cloned.1.call-done = f32[65536]{0:T(1024)} async-done(((f32[65536]{0:T(1024)}), f32[65536]{0:T(1024)}) %all-reduce.10.cloned.1.call-update) | async-done | bytes 262160
  890.1 1.6 dynamic-slice.5
  (158 shorter events, 32.5 us)
Async XLA Ops:
  7.2 42.7 %all-reduce.6.cloned.1.call-start = ((), (), s32[]{:S(2)}) async-start(), calls=%async_computation | async-start | bytes 524288 | tf_op jit(solution)/shard_map/psum | solution.py:55
  28.8 251.1 %all-gather.4.cloned.1.call-start = ((), (), s32[]{:S(2)}) async-start(), calls=%async_computation.1 | async-start | bytes 201326592 | tf_op jit(solution)/shard_map/all_gather | solution.py:59
  95.7 368.6 %all-reduce.8.cloned.1.call-start = ((), (), s32[]{:S(2)}) async-start(), calls=%async_computation.2 | async-start | bytes 4194304 | tf_op jit(solution)/shard_map/psum | solution.py:60
  361.1 106.4 %copy-start.1 = (s32[512,100]{0,1:T(8,128)S(1)}, s32[512,100]{0,1:T(8,128)}, u32[]{:S(2)}) copy-start(s32[512,100]{0,1:T(8,128)} %param.4) | copy-start | bytes 614404
  361.1 119.9 %all-gather.6.cloned.1.call-start = ((), (), s32[]{:S(2)}) async-start(), calls=%async_computation.3 | async-start | bytes 6291456 | tf_op jit(solution)/shard_map/all_gather | solution.py:62
  467.5 0.7 copy-start.2
  467.5 422.6 %all-reduce.10.cloned.1.call-start = ((), (), s32[]{:S(2)}) async-start(), calls=%async_computation.4 | async-start | bytes 524288
  499.4 1.9 copy-start
  838.7 31.0 %copy-start.3 = (f32[1024,1]{0,1:T(1,128)}, f32[1024,1]{0,1:T(1,128)S(1)}, u32[]{:S(2)}) copy-start(f32[1024,1]{0,1:T(1,128)S(1)} %constant_dynamic-update-slice_fusion.36) | copy-start | bytes 12292
  838.7 31.8 %copy-start.4 = (u32[32]{0:T(128)S(1)}, u32[32]{0:T(128)}, u32[]{:S(2)}) copy-start(u32[32]{0:T(128)} %constant.341) | copy-start | bytes 388
Sparse Core Ops, SparseCore 0:
  28.9 20.9 all-reduce.5
  95.8 183.9 all-gather.3
  361.3 102.9 all-reduce.7
  467.6 13.3 all-gather.5
  870.6 19.4 all-reduce.9
where the time goes:
time: 905 us; the launch traced here: 899 us
  waiting for transfers between devices  336 us (37%)
  other arithmetic  335 us (37%)
  matrix products  160 us (18%)
  local copies, waits for them, and re-layouts  42.7 us (5%)
  between operations  21.7 us (2%)
    all_gather x1, waiting for transfers between devices, local(): lax.all_gather(centred, 'smp', axis=0, tiled=True)  184 us
    another operation x30, other arithmetic, solve_system(): factor = jnp.linalg.cholesky(system)  167 us
    psum x1, waiting for transfers between devices, local(): gram_block = lax.psum(partial_rows, 'par') / NP  103 us
    another operation x3, other arithmetic, solve_system(): return jax.scipy.linalg.cho_solve((factor, True), centred_energy)  83.7 us
    dot_general x1, matrix products, row_products(): lax.dot_general(left, right, (((1,), (1,)), ((), ())), preferred_element_...  81.2 us
    convert_element_type x1, other arithmetic, local(): (log_derivs.astype(jnp.float32) - (col_sums / total_rows)[None, :]).astyp...  44.8 us
    dot_general x1, matrix products, back_project(): jnp.dot(weights, centred.astype(jnp.float32), precision=lax.Precision.HIG...  31 us
    another operation x14, matrix products, solve_system(): factor = jnp.linalg.cholesky(system)  27.2 us
  transfers between devices with their start and end apart: 5, of which 5 were waited for; matrix products, arithmetic and copies ran while one was open for 0% of the time, Pallas kernels for 0%

commit v1 on v0

v1 whole, which is shorter than its diff:
```python
import functools
import math

import jax
import jax.numpy as jnp
from jax import lax
from jax.experimental import pallas as pl
from jax.experimental.pallas import tpu as pltpu
from jax.sharding import PartitionSpec as P

NP = 524288
SIDE = 10


near_coupling = 1.0
diagonal_coupling = 0.5
damp_ratio = 0.05


def lattice_energy(spin_states):
    signs = (2 * spin_states - 1).astype(jnp.float32).reshape(spin_states.shape[0], SIDE, SIDE)
    nearest = signs * jnp.roll(signs, -1, 1) + signs * jnp.roll(signs, -1, 2)
    shifted = jnp.roll(signs, -1, 1)
    diagonal_pairs = signs * jnp.roll(shifted, -1, 2) + signs * jnp.roll(shifted, 1, 2)
    return near_coupling * jnp.sum(nearest, axis=(1, 2)) + diagonal_coupling * jnp.sum(
        diagonal_pairs, axis=(1, 2)
    )


HI = lax.Precision.HIGHEST
BLK = 128


def dot_f32(left, right, dims):
    return lax.dot_general(
        left, right, (dims, ((), ())), precision=HI, preferred_element_type=jnp.float32
    )


def factor_diagonal(work, inv_root):
    sub = lax.broadcasted_iota(jnp.int32, (8, BLK), 0)
    lane = lax.broadcasted_iota(jnp.int32, (8, BLK), 1)
    for r in range(0, BLK, 8):
        rows = work[r : r + 8, :]
        upper, side = rows[:, :BLK], rows[:, BLK:]
        cols = [jnp.broadcast_to(upper[:, r + j : r + j + 1], (8, BLK)) for j in range(8)]
        pivots = jnp.ones((8, BLK), jnp.float32)
        for j in range(8):
            recip = 1.0 / jnp.broadcast_to(cols[j][j : j + 1, :], (8, BLK))
            pivots = jnp.where(sub == j, recip, pivots)
            if j == 7:
                break
            ratio = jnp.where(sub > j, cols[j] * recip, 0.0)
            for l in range(j + 1, 8):
                cols[l] = cols[l] - ratio * cols[l][j : j + 1, :]
            upper = upper - ratio * upper[j : j + 1, :]
            side = side - ratio * side[j : j + 1, :]
        inv_root[r : r + 8, :] = side * jnp.sqrt(pivots)
        if r + 8 < BLK:
            scaled = jnp.where(lane >= r + 8, upper * pivots, 0.0)
            change = dot_f32(scaled, jnp.concatenate([upper, side], axis=1), ((0,), (0,)))
            work[r + 8 :, :] = work[r + 8 :, :] - change[r + 8 :, :]


def solve_kernel(gram_ref, energy_ref, out_ref, a, work, inv_roots):
    order = gram_ref.shape[0]
    blocks = order // BLK
    eye = jnp.where(
        lax.broadcasted_iota(jnp.int32, (BLK, BLK), 0)
        == lax.broadcasted_iota(jnp.int32, (BLK, BLK), 1),
        1.0,
        0.0,
    )
    diag = jnp.zeros((BLK, BLK), jnp.float32)
    for k in range(blocks):
        s = slice(k * BLK, (k + 1) * BLK)
        diag = diag + eye * gram_ref[s, s]
    damping = damp_ratio * (jnp.sum(diag) / order)
    a[...] = gram_ref[...]
    rhs = energy_ref[...]
    rhs = rhs - jnp.sum(rhs, axis=1, keepdims=True) / order
    solved = []
    for k in range(blocks):
        s = slice(k * BLK, (k + 1) * BLK)
        work[:, :BLK] = a[s, s] + damping * eye
        work[:, BLK:] = eye
        factor_diagonal(work, inv_roots.at[k])
        inv_root = inv_roots[k]
        y = dot_f32(rhs[:, :BLK], inv_root, ((1,), (1,)))
        solved.append(y)
        if k + 1 < blocks:
            panel = dot_f32(a[(k + 1) * BLK :, s], inv_root, ((1,), (1,)))
            a[(k + 1) * BLK :, s] = panel
            rhs = rhs[:, BLK:] - dot_f32(y, panel, ((1,), (1,)))
            for c in range(k + 1, blocks):
                t = slice(c * BLK, (c + 1) * BLK)
                a[c * BLK :, t] = a[c * BLK :, t] - dot_f32(
                    panel[(c - k - 1) * BLK :], panel[(c - k - 1) * BLK : (c - k) * BLK], ((1,), (1,))
                )
    below = None
    for k in reversed(range(blocks)):
        z = solved[k]
        if below is not None:
            z = z - dot_f32(below, a[(k + 1) * BLK :, k * BLK : (k + 1) * BLK], ((1,), (0,)))
        x = dot_f32(z, inv_roots[k], ((1,), (0,)))
        below = x if below is None else jnp.concatenate([x, below], axis=1)
    out_ref[...] = below


def solve_system(gram_matrix, energies):
    order = gram_matrix.shape[0]
    rows = jnp.broadcast_to(energies[None, :], (8, order))
    out = pl.pallas_call(
        solve_kernel,
        out_shape=jax.ShapeDtypeStruct((8, order), jnp.float32),
        in_specs=[pl.BlockSpec(memory_space=pltpu.VMEM)] * 2,
        out_specs=pl.BlockSpec(memory_space=pltpu.VMEM),
        scratch_shapes=[
            pltpu.VMEM((order, order), jnp.float32),
            pltpu.VMEM((BLK, 2 * BLK), jnp.float32),
            pltpu.VMEM((order // BLK, BLK, BLK), jnp.float32),
        ],
        compiler_params=pltpu.CompilerParams(vmem_limit_bytes=40 * 2**20),
        name="solve",
    )(gram_matrix, rows)
    return out[0]


def local(log_derivs, spin_states, offdiag_energy):
    row_count, width = log_derivs.shape
    cores = lax.axis_size("smp")
    total_rows = row_count * cores
    part = width // cores
    me = lax.axis_index("smp")
    local_energy = lattice_energy(spin_states) + offdiag_energy
    energies = lax.all_gather(local_energy, "smp", axis=0, tiled=True)
    own = lax.dynamic_slice_in_dim(log_derivs, me * part, part, 1)
    theirs = lax.dynamic_slice_in_dim(log_derivs, (1 - me) * part, part, 1)
    got = lax.ppermute(theirs, "smp", [(0, 1), (1, 0)])
    first = jnp.where(me == 0, own, got)
    second = jnp.where(me == 0, got, own)
    rows = jnp.concatenate([first, second], axis=0)
    means = jnp.sum(rows.astype(jnp.float32), axis=0) / total_rows
    centred = (rows.astype(jnp.float32) - means[None, :]).astype(jnp.bfloat16)
    partial_gram = lax.dot_general(
        centred, centred, (((1,), (1,)), ((), ())), preferred_element_type=jnp.float32
    )
    gram_matrix = lax.psum(partial_gram, ("par", "smp")) / NP
    coefficients = solve_system(gram_matrix, energies)
    param_update = -jnp.dot(
        coefficients,
        centred.astype(jnp.float32),
        precision=lax.Precision.HIGHEST,
        preferred_element_type=jnp.float32,
    ) / math.sqrt(total_rows)
    return (param_update, coefficients)


def solution(mesh):
    placed = (P(("grp", "smp"), "par"), P(("grp", "smp"), None), P(("grp", "smp")))
    return jax.shard_map(
        local,
        mesh=mesh,
        in_specs=placed,
        out_specs=(P(("grp", "par", "smp")), P("grp")),
        check_vma=False,
    )
```

time: 905 us -> 478 us (0.53)
  other arithmetic: 335 us -> 69.5 us
  waiting for transfers between devices: 336 us -> 160 us
  Pallas kernels: 0 us -> 82.1 us
  matrix products: 160 us -> 121 us
  local copies, waits for them, and re-layouts: 42.7 us -> 23.6 us
    another operation x33 -> x0, other arithmetic: 251 us -> none  [the longest x30 167 us: solve_system(): factor = jnp.linalg.cholesky(system)]
    all_gather x2 -> x0, waiting for transfers between devices: 194 us -> none  [the longest x1 184 us: local(): lax.all_gather(centred, 'smp', axis=0, tiled=True)]
    pallas_call x0 -> x1, Pallas kernels: none -> 82.1 us  [solve_system(): pl.pallas_call(solve_kernel, out_shape=jax.ShapeDtypeStruct((8, order), j...]
    ppermute x0 -> x1, waiting for transfers between devices: none -> 49.1 us  [local(): got = lax.ppermute(theirs, 'smp', [(0, 1), (1, 0)])]
    another operation x44 -> x0, matrix products: 47.8 us -> none  [the longest x14 27.2 us: solve_system(): factor = jnp.linalg.cholesky(system)]
    convert_element_type x1 -> x0, other arithmetic: 44.8 us -> none  [local(): (log_derivs.astype(jnp.float32) - (col_sums / total_rows)[None, :]).astyp...]
    select_n x0 -> x1, other arithmetic: none -> 44.5 us  [local(): first = jnp.where(me == 0, own, got)]
    another operation x70 -> x0, local copies, waits for them, and re-layouts: 32.6 us -> none
  transfers between devices with their start and end apart: 5 -> 2, of which waited for: 5 -> 2; matrix products, arithmetic and copies ran while one was open for 0% -> 0% of each run, Pallas kernels for 0% -> 0%
where the time goes in v1:
time: 478 us; the launch traced here: 474 us
  waiting for transfers between devices  160 us (33%)
  matrix products  121 us (25%)
  Pallas kernels  82.1 us (17%)
  other arithmetic  69.5 us (15%)
  local copies, waits for them, and re-layouts  23.6 us (5%)
  between operations  14.6 us (3%)
    psum x1, waiting for transfers between devices, local(): gram_matrix = lax.psum(partial_gram, ('par', 'smp')) / NP  111 us
    dot_general x1, matrix products, local(): lax.dot_general(centred, centred, (((1,), (1,)), ((), ())), preferred_ele...  85 us
    pallas_call x1, Pallas kernels, solve_system(): pl.pallas_call(solve_kernel, out_shape=jax.ShapeDtypeStruct((8, order), j...  82.1 us
    ppermute x1, waiting for transfers between devices, local(): got = lax.ppermute(theirs, 'smp', [(0, 1), (1, 0)])  49.1 us
    select_n x1, other arithmetic, local(): first = jnp.where(me == 0, own, got)  44.5 us
    dot_general x1, matrix products, local(): jnp.dot(coefficients, centred.astype(jnp.float32), precision=lax.Precisio...  35.6 us
    dynamic_slice x1, local copies, waits for them, and re-layouts, local(): theirs = lax.dynamic_slice_in_dim(log_derivs, (1 - me) * part, part, 1)  22.9 us
    reduce_sum x1, other arithmetic, local(): means = jnp.sum(rows.astype(jnp.float32), axis=0) / total_rows  21 us
  transfers between devices with their start and end apart: 2, of which 2 were waited for; matrix products, arithmetic and copies ran while one was open for 0% of the time, Pallas kernels for 0%

profile of v1, /device:TPU:0, one launch (start us, length us, event | category | flops | bytes accessed | tf_op | source)
XLA Modules:
  0.0 473.7 jit_solution(7262679191579642770)
XLA Ops:
  7.2 0.0 all-reduce.2.cloned.1.call-start
  7.2 22.9 %constant_dynamic-slice_fusion = bf16[512,32768]{1,0:T(8,128)(2,1)} fusion(bf16[512,65536]{1,0:T(8,128)(2,1)} %param.3, s32[]{:T(128)S(6)} %select_n.20), kind=kLoop, calls=%fused_computation.29 | loop fusion | bytes 67108864 | tf_op jit(solution)/shard_map/dynamic_slice | solution.py:138
  30.1 0.5 collective-permute-start
  30.5 49.1 %collective-permute-done = bf16[512,32768]{1,0:T(8,128)(2,1)} collective-permute-done((bf16[512,32768]{1,0:T(8,128)(2,1)}, bf16[512,32768]{1,0:T(8,128)(2,1)}, u32[]{:S(2)}, u32[]{:S(2)}) %collective-permute-start) | collective-permute-done | bytes 33554464 | tf_op jit(solution)/shard_map/ppermute | solution.py:139
  79.7 44.5 %broadcast_select_fusion.1 = (bf16[512,32768]{1,0:T(8,128)(2,1)}, bf16[512,32768]{1,0:T(8,128)(2,1)}) fusion(bf16[512,32768]{1,0:T(8,128)(2,1)} %collective-permute-done, pred[]{:T(512)S(6)} %eq.4, bf16[512,65536]{1,0:T(8,128)(2,1)} %param.3, s32[]{:T(128)S(6)} %select_n.19), kind=kLoop, calls=%fused_computation.7 | loop fusion | flops 33554432 | bytes 134217728 | tf_op jit(solution)/shard_map/jit(_where)/select_n | solution.py:140
  124.1 21.0 %convert_reduce_fusion = f32[32768]{0:T(1024)S(1)} fusion(bf16[512,32768]{1,0:T(8,128)(2,1)} %get-tuple-element.5, bf16[512,32768]{1,0:T(8,128)(2,1)} %get-tuple-element.4), kind=kLoop, calls=%fused_computation.1 | loop fusion | flops 167739392 | bytes 67239936 | tf_op jit(solution)/shard_map/reduce_sum | solution.py:143
  145.1 0.0 copy-start
  145.1 0.0 copy-start.1
  145.1 85.0 %fusion.3 = f32[1024,1024]{1,0:T(8,128)} fusion(f32[32768]{0:T(1024)S(1)} %broadcast_multiply_fusion.1, bf16[512,32768]{1,0:T(8,128)(2,1)} %get-tuple-element.5, bf16[512,32768]{1,0:T(8,128)(2,1)} %get-tuple-element.4), kind=kOutput, calls=%fused_computation.5 | convolution fusion | flops 68920803328 | bytes 71434240 | tf_op jit(solution)/shard_map/dot_general | solution.py:145
  230.1 0.0 all-reduce.2.cloned.1.call-update
  230.2 0.0 copy-done
  230.4 0.1 fusion.7
  230.5 0.1 maximum_add_fusion
  230.6 0.1 fusion.5
  230.7 0.1 multiply_reduce_fusion
  230.8 0.0 copy-done.1
  230.8 2.3 all-gather
  233.1 111.3 %all-reduce.2.cloned.1.call-done = f32[1024,1024]{1,0:T(8,128)} async-done(((f32[1024,1024]{1,0:T(8,128)}), f32[1024,1024]{1,0:T(8,128)}) %all-reduce.2.cloned.1.call-update) | async-done | bytes 4194320 | tf_op jit(solution)/shard_map/psum | solution.py:148
  344.4 3.0 broadcast_multiply_fusion.gram_ref
  347.4 82.1 %solve.1 = f32[8,1024]{1,0:T(8,128)S(1)} custom-call(f32[1024,1024]{1,0:T(8,128)S(1)} %broadcast_multiply_fusion.gram_ref, f32[8,1024]{1,0:T(8,128)S(1)} %broadcast_in_dim.2.energy_ref), custom_call_target="tpu_custom_call" | custom-call | tf_op jit(solution)/shard_map/solve/pallas_call | solution.py:113
  429.5 35.6 %fusion.1 = f32[1,32768]{1,0:T(1,128)S(1)} fusion(f32[32768]{0:T(1024)S(1)} %broadcast_multiply_fusion.1, bf16[512,32768]{1,0:T(8,128)(2,1)} %get-tuple-element.5, bf16[512,32768]{1,0:T(8,128)(2,1)} %get-tuple-element.4, f32[8,1024]{1,0:T(8,128)S(1)} %solve.1), kind=kOutput, calls=%fused_computation.4 | convolution fusion | flops 603979776 | bytes 67375104 | tf_op jit(solution)/shard_map/dot_general | solution.py:150
  465.1 0.6 slice.56
  465.7 0.7 negate_multiply_fusion
  (12 shorter events, 0.2 us)
Async XLA Ops:
  7.2 337.2 %all-reduce.2.cloned.1.call-start = ((), (), s32[]{:S(2)}) async-start(), calls=%async_computation | async-start | bytes 8388608 | tf_op jit(solution)/shard_map/psum | solution.py:148
  30.1 49.6 %collective-permute-start = (bf16[512,32768]{1,0:T(8,128)(2,1)}, bf16[512,32768]{1,0:T(8,128)(2,1)}, u32[]{:S(2)}, u32[]{:S(2)}) collective-permute-start(bf16[512,32768]{1,0:T(8,128)(2,1)} %constant_dynamic-slice_fusion), channel_id=1, source_target_pairs={{0,1},{1,0},{2,3},{3,2},{4,5},{5,4},{6,7},{7,6},{8,9},{9,8},{10,11... | collective-permute-start | bytes 100663304 | tf_op jit(solution)/shard_map/ppermute | solution.py:139
  145.1 85.1 %copy-start = (s32[512,100]{0,1:T(8,128)S(1)}, s32[512,100]{0,1:T(8,128)}, u32[]{:S(2)}) copy-start(s32[512,100]{0,1:T(8,128)} %param.4) | copy-start | bytes 614404
  145.1 85.7 %copy-start.1 = (f32[512]{0:T(512)S(1)}, f32[512]{0:T(512)}, u32[]{:S(2)}) copy-start(f32[512]{0:T(512)} %param.5) | copy-start | bytes 6148
Sparse Core Ops, SparseCore 0:
  230.3 114.0 all-reduce.1

commit v2 on v1

--- a/solution.py
+++ b/solution.py
@@ -25,6 +25,103 @@
     return near_coupling * jnp.sum(nearest, axis=(1, 2)) + diagonal_coupling * jnp.sum(
         diagonal_pairs, axis=(1, 2)
     )
+
+
+TILE = 256
+WIDE = 2048
+SUB = 512
+
+
+def block_pairs(order):
+    return [(i, j) for i in range(order // TILE) for j in range(i + 1)]
+
+
+def gram_kernel(me_ref, own_ref, got_ref, start_ref, centred_ref, gram_ref):
+    rows = own_ref.shape[0]
+    me = me_ref[0]
+    own_at = pl.ds(pl.multiple_of(me * rows, rows), rows)
+    got_at = pl.ds(pl.multiple_of((1 - me) * rows, rows), rows)
+
+    @pl.when(pl.program_id(0) == 0)
+    def _():
+        gram_ref[...] = start_ref[...]
+
+    def centre(n):
+        at = slice(n * SUB, (n + 1) * SUB)
+        own = own_ref[:, at].astype(jnp.float32)
+        got = got_ref[:, at].astype(jnp.float32)
+        sums = jnp.sum(own, axis=0, keepdims=True) + jnp.sum(got, axis=0, keepdims=True)
+        means = sums / (2 * rows)
+        centred_ref[own_at, at] = (own - means).astype(jnp.bfloat16)
+        centred_ref[got_at, at] = (got - means).astype(jnp.bfloat16)
+
+    count = own_ref.shape[1] // SUB
+    for n in range(count):
+        centre(n)
+    for b, (i, j) in enumerate(block_pairs(2 * rows)):
+        gram_ref[b] += lax.dot_general(
+            centred_ref[i * TILE : (i + 1) * TILE, :],
+            centred_ref[j * TILE : (j + 1) * TILE, :],
+            (((1,), (1,)), ((), ())),
+            preferred_element_type=jnp.float32,
+        )
+
+
+def add_gram(me, log_derivs, got, start, first_block):
+    rows, width = got.shape
+    total = 2 * rows
+    per_core = log_derivs.shape[1] // 2 // WIDE
+    return pl.pallas_call(
+        gram_kernel,
+        grid_spec=pltpu.PrefetchScalarGridSpec(
+            num_scalar_prefetch=1,
+            grid=(width // WIDE,),
+            in_specs=[
+                pl.BlockSpec((rows, WIDE), lambda n, me: (0, me[0] * per_core + first_block + n)),
+                pl.BlockSpec((rows, WIDE), lambda n, me: (0, n)),
+                pl.BlockSpec(start.shape, lambda n, me: (0, 0, 0)),
+            ],
+            out_specs=[
+                pl.BlockSpec((total, WIDE), lambda n, me: (0, n)),
+                pl.BlockSpec(start.shape, lambda n, me: (0, 0, 0)),
+            ],
+        ),
+        out_shape=[
+            jax.ShapeDtypeStruct((total, width), jnp.bfloat16),
+            jax.ShapeDtypeStruct(start.shape, jnp.float32),
+        ],
+        compiler_params=pltpu.CompilerParams(vmem_limit_bytes=50 * 2**20),
+        cost_estimate=pl.CostEstimate(
+            flops=int(1.3 * total * total * width), bytes_accessed=8 * rows * width, transcendentals=0
+        ),
+        name="gram",
+    )(me.reshape(1), log_derivs, got, start)
+
+
+def update_kernel(centred_ref, coeffs_ref, out_ref):
+    rows, width = centred_ref.shape
+    total = jnp.zeros((16, width), jnp.float32)
+    for r in range(0, rows, 16):
+        weights = jnp.concatenate([coeffs_ref[r : r + 16, :]] * (width // 128), axis=1)
+        total = total + weights * centred_ref[r : r + 16, :].astype(jnp.float32)
+    out_ref[...] = jnp.sum(total, axis=0, keepdims=True) * (-1.0 / math.sqrt(rows))
+
+
+def back_project(coeffs, centred):
+    rows, width = centred.shape
+    tile = 1024
+    return pl.pallas_call(
+        update_kernel,
+        grid=(width // tile,),
+        in_specs=[
+            pl.BlockSpec((rows, tile), lambda n: (0, n)),
+            pl.BlockSpec((rows, 128), lambda n: (0, 0)),
+        ],
+        out_specs=pl.BlockSpec((1, tile), lambda n: (0, n)),
+        out_shape=jax.ShapeDtypeStruct((1, width), jnp.float32),
+        compiler_params=pltpu.CompilerParams(vmem_limit_bytes=40 * 2**20),
+        name="update",
+    )(centred, coeffs)[0]
 
 
 HI = lax.Precision.HIGHEST
@@ -63,8 +160,10 @@
 
 
 def solve_kernel(gram_ref, energy_ref, out_ref, a, work, inv_roots):
-    order = gram_ref.shape[0]
+    order = a.shape[0]
     blocks = order // BLK
+    for b, (i, j) in enumerate(block_pairs(order)):
+        a[i * TILE : (i + 1) * TILE, j * TILE : (j + 1) * TILE] = gram_ref[b] / NP
     eye = jnp.where(
         lax.broadcasted_iota(jnp.int32, (BLK, BLK), 0)
         == lax.broadcasted_iota(jnp.int32, (BLK, BLK), 1),
@@ -74,9 +173,8 @@
     diag = jnp.zeros((BLK, BLK), jnp.float32)
     for k in range(blocks):
         s = slice(k * BLK, (k + 1) * BLK)
-        diag = diag + eye * gram_ref[s, s]
+        diag = diag + eye * a[s, s]
     damping = damp_ratio * (jnp.sum(diag) / order)
-    a[...] = gram_ref[...]
     rhs = energy_ref[...]
     rhs = rhs - jnp.sum(rhs, axis=1, keepdims=True) / order
     solved = []
@@ -107,8 +205,8 @@
     out_ref[...] = below
 
 
-def solve_system(gram_matrix, energies):
-    order = gram_matrix.shape[0]
+def solve_system(gram_blocks, energies):
+    order = energies.shape[0]
     rows = jnp.broadcast_to(energies[None, :], (8, order))
     out = pl.pallas_call(
         solve_kernel,
@@ -122,7 +220,7 @@
         ],
         compiler_params=pltpu.CompilerParams(vmem_limit_bytes=40 * 2**20),
         name="solve",
-    )(gram_matrix, rows)
+    )(gram_blocks, rows)
     return out[0]
 
 
@@ -134,25 +232,21 @@
     me = lax.axis_index("smp")
     local_energy = lattice_energy(spin_states) + offdiag_energy
     energies = lax.all_gather(local_energy, "smp", axis=0, tiled=True)
-    own = lax.dynamic_slice_in_dim(log_derivs, me * part, part, 1)
-    theirs = lax.dynamic_slice_in_dim(log_derivs, (1 - me) * part, part, 1)
-    got = lax.ppermute(theirs, "smp", [(0, 1), (1, 0)])
-    first = jnp.where(me == 0, own, got)
-    second = jnp.where(me == 0, got, own)
-    rows = jnp.concatenate([first, second], axis=0)
-    means = jnp.sum(rows.astype(jnp.float32), axis=0) / total_rows
-    centred = (rows.astype(jnp.float32) - means[None, :]).astype(jnp.bfloat16)
-    partial_gram = lax.dot_general(
-        centred, centred, (((1,), (1,)), ((), ())), preferred_element_type=jnp.float32
-    )
-    gram_matrix = lax.psum(partial_gram, ("par", "smp")) / NP
-    coefficients = solve_system(gram_matrix, energies)
-    param_update = -jnp.dot(
-        coefficients,
-        centred.astype(jnp.float32),
-        precision=lax.Precision.HIGHEST,
-        preferred_element_type=jnp.float32,
-    ) / math.sqrt(total_rows)
+    chunks = min(4, part // WIDE)
+    chunk = part // chunks
+    got = []
+    for n in range(chunks):
+        theirs = lax.dynamic_slice_in_dim(log_derivs, (1 - me) * part + n * chunk, chunk, 1)
+        got.append(lax.ppermute(theirs, "smp", [(0, 1), (1, 0)]))
+    gram_blocks = jnp.zeros((len(block_pairs(total_rows)), TILE, TILE), jnp.float32)
+    pieces = []
+    for n in range(chunks):
+        centred, gram_blocks = add_gram(me, log_derivs, got[n], gram_blocks, n * chunk // WIDE)
+        pieces.append(centred)
+    gram_blocks = lax.psum(gram_blocks, ("par", "smp"))
+    coefficients = solve_system(gram_blocks, energies)
+    coeffs = jnp.broadcast_to(coefficients[:, None], (total_rows, 128))
+    param_update = jnp.concatenate([back_project(coeffs, piece) for piece in pieces])
     return (param_update, coefficients)
 
 

time: 478 us -> 390 us (0.82)
  Pallas kernels: 82.1 us -> 216 us
  matrix products: 121 us -> 0 us
  other arithmetic: 69.5 us -> 1.02 us
  waiting for transfers between devices: 160 us -> 119 us
  local copies, waits for them, and re-layouts: 23.6 us -> 28.9 us
    pallas_call x0 -> x8, Pallas kernels: none -> 134 us  [the longest x4 97 us: add_gram(): pl.pallas_call(gram_kernel, grid_spec=pltpu.PrefetchScalarGridSpec(num_sc...]
    dot_general x2 -> x0, matrix products: 121 us -> none  [the longest x1 85 us: local(): lax.dot_general(centred, centred, (((1,), (1,)), ((), ())), preferred_ele...]
    select_n x1 -> x0, other arithmetic: 44.5 us -> none  [local(): first = jnp.where(me == 0, own, got)]
    ppermute x1 -> x4, waiting for transfers between devices: 49.1 us -> 18.8 us  [local(): got.append(lax.ppermute(theirs, 'smp', [(0, 1), (1, 0)]))]
    reduce_sum x1 -> x0, other arithmetic: 21 us -> none  [local(): means = jnp.sum(rows.astype(jnp.float32), axis=0) / total_rows]
    psum x1, waiting for transfers between devices: 111 us -> 100 us  [local(): gram_blocks = lax.psum(gram_blocks, ('par', 'smp'))]
    unnamed x4 -> x14, local copies, waits for them, and re-layouts: 0.01 us -> 6.45 us
  transfers between devices with their start and end apart: 2 -> 5, of which waited for: 2 -> 2; matrix products, arithmetic and copies ran while one was open for 0% -> 1% of each run, Pallas kernels for 0% -> 19%
where the time goes in v2:
time: 390 us; the launch traced here: 383 us
  Pallas kernels  216 us (55%)
  waiting for transfers between devices  119 us (31%)
  local copies, waits for them, and re-layouts  28.9 us (7%)
  between operations  14.7 us (4%)
    psum x1, waiting for transfers between devices, local(): gram_blocks = lax.psum(gram_blocks, ('par', 'smp'))  100 us
    pallas_call x4, Pallas kernels, add_gram(): pl.pallas_call(gram_kernel, grid_spec=pltpu.PrefetchScalarGridSpec(num_sc...  97 us
    pallas_call x1, Pallas kernels, solve_system(): pl.pallas_call(solve_kernel, out_shape=jax.ShapeDtypeStruct((8, order), j...  82.1 us
    pallas_call x4, Pallas kernels, back_project(): pl.pallas_call(update_kernel, grid=(width // tile,), in_specs=[pl.BlockSp...  36.7 us
    dynamic_slice x1, local copies, waits for them, and re-layouts, local(): lax.dynamic_slice_in_dim(log_derivs, (1 - me) * part + n * chunk, chunk, 1)  20.2 us
    ppermute x4, waiting for transfers between devices, local(): got.append(lax.ppermute(theirs, 'smp', [(0, 1), (1, 0)]))  18.8 us
  transfers between devices with their start and end apart: 5, of which 2 were waited for; matrix products, arithmetic and copies ran while one was open for 1% of the time, Pallas kernels for 19%

profile of v2, /device:TPU:0, one launch (start us, length us, event | category | flops | bytes accessed | tf_op | source)
XLA Modules:
  0.0 382.9 jit_solution(6467138546334177914)
XLA Ops:
  7.2 0.0 all-reduce.2.cloned.1.call-start
  7.2 20.2 %constant_dynamic-slice_fusion.3 = (bf16[512,8192]{1,0:T(8,128)(2,1)}, bf16[512,8192]{1,0:T(8,128)(2,1)}, bf16[512,8192]{1,0:T(8,128)(2,1)}, bf16[512,8192]{1,0:T(8,128)(2,1)S(1)}) fusion(bf16[512,65536]{1,0:T(8,128)(2,1)} %own_ref.7, s32[]{:T(128)S(6)} %select_n.12, s32[]{:T(128)S(6)} %select_n.15, s32[]{:T(128)S(6)} %select_n.14, s32[]{:T(128)S(6)} %select_n.13), kind=kLoop, calls=%fused_computation.21 | loop fusion | bytes 67108880 | tf_op jit(solution)/shard_map/dynamic_slice | solution.py:239
  27.5 0.5 collective-permute-start
  27.9 0.1 collective-permute-start.3
  28.0 0.4 collective-permute-start.2
  28.4 0.1 collective-permute-start.1
  28.5 18.8 %collective-permute-done.got_ref = bf16[512,8192]{1,0:T(8,128)(2,1)} collective-permute-done((bf16[512,8192]{1,0:T(8,128)(2,1)}, bf16[512,8192]{1,0:T(8,128)(2,1)}, u32[]{:S(2)}, u32[]{:S(2)}) %collective-permute-start) | collective-permute-done | bytes 8388640 | tf_op jit(solution)/shard_map/ppermute | solution.py:240
  47.3 1.8 broadcast_in_dim.16.start_ref
  49.1 23.8 %gram.4 = (bf16[1024,8192]{1,0:T(8,128)(2,1)}, f32[10,256,256]{2,1,0:T(8,128)S(1)}) custom-call(s32[1]{0:T(128)} %bitcast.me_ref, bf16[512,65536]{1,0:T(8,128)(2,1)} %own_ref.7, bf16[512,8192]{1,0:T(8,128)(2,1)} %collective-permute-done.got_ref, f32[10,256,256]{2,1,0:T(8,128)} %broadcast_in_dim.16.start_ref), custom_call_target="tpu_custom_call" | custom-call | flops 11166914560 | bytes 33554432 | tf_op jit(solution)/shard_map/gram/pallas_call | solution.py:74
  72.9 0.0 copy-start.1
  72.9 1.5 copy-done.1
  74.4 0.0 collective-permute-done.3.got_ref
  74.4 23.8 %gram.5 = (bf16[1024,8192]{1,0:T(8,128)(2,1)}, f32[10,256,256]{2,1,0:T(8,128)S(1)}) custom-call(s32[1]{0:T(128)} %bitcast.me_ref, bf16[512,65536]{1,0:T(8,128)(2,1)} %own_ref.7, bf16[512,8192]{1,0:T(8,128)(2,1)} %collective-permute-done.3.got_ref, f32[10,256,256]{2,1,0:T(8,128)} %copy-done.1), custom_call_target="tpu_custom_call" | custom-call | flops 11166914560 | bytes 33554432 | tf_op jit(solution)/shard_map/gram/pallas_call | solution.py:74
  98.2 0.0 copy-start.2
  98.2 1.5 copy-done.2
  99.7 0.0 collective-permute-done.2.got_ref
  99.7 24.0 %gram.6 = (bf16[1024,8192]{1,0:T(8,128)(2,1)}, f32[10,256,256]{2,1,0:T(8,128)S(1)}) custom-call(s32[1]{0:T(128)} %bitcast.me_ref, bf16[512,65536]{1,0:T(8,128)(2,1)} %own_ref.7, bf16[512,8192]{1,0:T(8,128)(2,1)} %collective-permute-done.2.got_ref, f32[10,256,256]{2,1,0:T(8,128)} %copy-done.2), custom_call_target="tpu_custom_call" | custom-call | flops 11166914560 | bytes 33554432 | tf_op jit(solution)/shard_map/gram/pallas_call | solution.py:74
  123.8 0.0 copy-start
  123.8 1.7 copy-done
  125.5 0.0 collective-permute-done.1.got_ref
  125.5 0.0 copy-start.4
  125.5 25.3 %gram.7 = (bf16[1024,8192]{1,0:T(8,128)(2,1)}, f32[10,256,256]{2,1,0:T(8,128)}) custom-call(s32[1]{0:T(128)} %bitcast.me_ref, bf16[512,65536]{1,0:T(8,128)(2,1)} %own_ref.7, bf16[512,8192]{1,0:T(8,128)(2,1)} %collective-permute-done.1.got_ref, f32[10,256,256]{2,1,0:T(8,128)} %copy-done), custom_call_target="tpu_custom_call" | custom-call | flops 11166914560 | bytes 33554432 | tf_op jit(solution)/shard_map/gram/pallas_call | solution.py:74
  150.8 0.0 copy-start.6
  150.8 0.0 all-reduce.2.cloned.1.call-update
  150.8 0.0 copy-done.4
  151.0 0.1 fusion.2
  151.1 0.1 maximum_add_fusion
  151.2 0.1 fusion
  151.3 0.1 multiply_reduce_fusion
  151.4 0.0 copy-done.6
  151.4 2.2 all-gather
  153.7 100.5 %all-reduce.2.cloned.1.call-done.gram_ref = f32[10,256,256]{2,1,0:T(8,128)} async-done(((f32[10,256,256]{2,1,0:T(8,128)}), f32[10,256,256]{2,1,0:T(8,128)}) %all-reduce.2.cloned.1.call-update) | async-done | bytes 2621456 | tf_op jit(solution)/shard_map/psum | solution.py:246
  254.2 0.0 copy-start.3
  254.2 1.7 copy-done.3
  255.9 82.1 %solve.1 = f32[8,1024]{1,0:T(8,128)S(1)} custom-call(f32[10,256,256]{2,1,0:T(8,128)S(1)} %copy-done.3, f32[8,1024]{1,0:T(8,128)S(1)} %broadcast_in_dim.17.energy_ref), custom_call_target="tpu_custom_call" | custom-call | tf_op jit(solution)/shard_map/solve/pallas_call | solution.py:211
  338.0 0.0 copy-start.5
  338.0 0.2 broadcast_in_dim.19.coeffs_ref
  338.2 9.2 %update.4 = f32[1,8192]{1,0:T(1,128)S(1)} custom-call(bf16[1024,8192]{1,0:T(8,128)(2,1)} %get-tuple-element.10.centred_ref, f32[1024,128]{1,0:T(8,128)S(1)} %broadcast_in_dim.19.coeffs_ref), custom_call_target="tpu_custom_call" | custom-call | tf_op jit(solution)/shard_map/update/pallas_call | solution.py:113
  347.4 0.0 copy-done.5
  347.4 9.2 %update.5 = f32[1,8192]{1,0:T(1,128)S(1)} custom-call(bf16[1024,8192]{1,0:T(8,128)(2,1)} %get-tuple-element.15.centred_ref, f32[1024,128]{1,0:T(8,128)S(1)} %broadcast_in_dim.19.coeffs_ref), custom_call_target="tpu_custom_call" | custom-call | tf_op jit(solution)/shard_map/update/pallas_call | solution.py:113
  356.6 9.2 %update.6 = f32[1,8192]{1,0:T(1,128)S(1)} custom-call(bf16[1024,8192]{1,0:T(8,128)(2,1)} %get-tuple-element.16.centred_ref, f32[1024,128]{1,0:T(8,128)S(1)} %broadcast_in_dim.19.coeffs_ref), custom_call_target="tpu_custom_call" | custom-call | tf_op jit(solution)/shard_map/update/pallas_call | solution.py:113
  365.8 9.2 %update.7 = f32[1,8192]{1,0:T(1,128)S(1)} custom-call(bf16[1024,8192]{1,0:T(8,128)(2,1)} %get-tuple-element.17.centred_ref, f32[1024,128]{1,0:T(8,128)S(1)} %broadcast_in_dim.19.coeffs_ref), custom_call_target="tpu_custom_call" | custom-call | tf_op jit(solution)/shard_map/update/pallas_call | solution.py:113
  375.0 0.7 pad_maximum_fusion.1
  (12 shorter events, 0.2 us)
Async XLA Ops:
  7.2 247.0 %all-reduce.2.cloned.1.call-start = ((), (), s32[]{:S(2)}) async-start(), calls=%async_computation | async-start | bytes 5242880 | tf_op jit(solution)/shard_map/psum | solution.py:246
  27.5 19.8 %collective-permute-start = (bf16[512,8192]{1,0:T(8,128)(2,1)}, bf16[512,8192]{1,0:T(8,128)(2,1)}, u32[]{:S(2)}, u32[]{:S(2)}) collective-permute-start(bf16[512,8192]{1,0:T(8,128)(2,1)} %get-tuple-element.20), channel_id=1, source_target_pairs={{0,1},{1,0},{2,3},{3,2},{4,5},{5,4},{6,7},{7,6},{8,9},{9,8},{10,11... | collective-permute-start | bytes 25165832 | tf_op jit(solution)/shard_map/ppermute | solution.py:240
  27.9 46.5 %collective-permute-start.3 = (bf16[512,8192]{1,0:T(8,128)(2,1)}, bf16[512,8192]{1,0:T(8,128)(2,1)}, u32[]{:S(2)}, u32[]{:S(2)}) collective-permute-start(bf16[512,8192]{1,0:T(8,128)(2,1)} %get-tuple-element.21), channel_id=1, source_target_pairs={{0,1},{1,0},{2,3},{3,2},{4,5},{5,4},{6,7},{7,6},{8,9},{9,8},{10,11... | collective-permute-start | bytes 25165832 | tf_op jit(solution)/shard_map/ppermute | solution.py:240
  28.0 71.8 %collective-permute-start.2 = (bf16[512,8192]{1,0:T(8,128)(2,1)}, bf16[512,8192]{1,0:T(8,128)(2,1)}, u32[]{:S(2)}, u32[]{:S(2)}) collective-permute-start(bf16[512,8192]{1,0:T(8,128)(2,1)} %get-tuple-element.22), channel_id=1, source_target_pairs={{0,1},{1,0},{2,3},{3,2},{4,5},{5,4},{6,7},{7,6},{8,9},{9,8},{10,11... | collective-permute-start | bytes 25165832 | tf_op jit(solution)/shard_map/ppermute | solution.py:240
  28.4 97.0 %collective-permute-start.1 = (bf16[512,8192]{1,0:T(8,128)(2,1)S(1)}, bf16[512,8192]{1,0:T(8,128)(2,1)}, u32[]{:S(2)}, u32[]{:S(2)}) collective-permute-start(bf16[512,8192]{1,0:T(8,128)(2,1)S(1)} %get-tuple-element.23), channel_id=1, source_target_pairs={{0,1},{1,0},{2,3},{3,2},{4,5},{5,4},{6,7},{7,6},{8,9},{9,8},{10,11... | collective-permute-start | bytes 25165832 | tf_op jit(solution)/shard_map/ppermute | solution.py:240
  72.9 1.5 copy-start.1
  98.2 1.5 copy-start.2
  123.8 1.7 copy-start
  125.5 25.3 %copy-start.4 = (s32[512,100]{0,1:T(8,128)S(1)}, s32[512,100]{0,1:T(8,128)}, u32[]{:S(2)}) copy-start(s32[512,100]{0,1:T(8,128)} %param.4) | copy-start | bytes 614404
  150.8 0.7 copy-start.6
  254.2 1.7 copy-start.3
  338.0 9.4 %copy-start.5 = (f32[1,1024]{1,0:T(1,128)}, f32[1,1024]{1,0:T(1,128)S(1)}, u32[]{:S(2)}) copy-start(f32[1,1024]{1,0:T(1,128)S(1)} %slice.56) | copy-start | bytes 12292
Sparse Core Ops, SparseCore 0:
  150.9 103.2 all-reduce.1
